TPU v7x, 32 devices: a whole 2x2x4 slice. The times are simulated.
32 devices in a mesh: parts: 2 (over y), blk: 4 (over z), tp: 2 (over x), sub: 2 (over core).
Axes of the slice: x: 2, y: 2, z: 4, core: 2. Of those that a mesh axis runs over, the one named last changes fastest.
Arguments:
- inputs: bfloat16 [2048, 4096], P(('parts', 'blk')), parts along dimension 0, may hold values from -20 to 20
- context_gradient: bfloat16 [2048, 4096], P(('parts', 'blk'), ('tp', 'sub')), parts along dimension 0, may hold values from -6 to 6
- positions: int32 [2048], P(('parts', 'blk')), parts along dimension 0, may hold values from 0 to 255, as said below
- query_weight: bfloat16 [4096, 4096], P('blk', ('tp', 'sub')), may hold values from -0.09375 to 0.09375
- key_value_weight: bfloat16 [4096, 2, 1024], P('blk', 'sub', 'tp'), may hold values from -0.09375 to 0.09375
Outputs:
- grad_inputs: bfloat16 [2048, 4096], P(('parts', 'blk'), ('tp', 'sub')), parts along dimension 0
- grad_query: bfloat16 [8192, 4096], P(('parts', 'blk'), ('tp', 'sub')), parts along dimension 0
- grad_keyval: bfloat16 [8192, 2, 1024], P(('parts', 'blk'), 'sub', 'tp'), parts along dimension 0
There are 2 independent parts, one for each index of `parts`. A program takes and returns all parts, laid end to end along the dimension named above; an argument that names none is the same for every part. Nothing has to cross between parts.
Inputs may be any that keep to these rules, and one draw needn't show every extreme that they name: `positions`: each aligned block of 256 tokens holds whole sequences in order: a position is 0 where a sequence starts and one more than the previous token's otherwise; the first block is one sequence.
All inputs are finite; a program needn't handle non-finite values.
Results may differ from a plain program's by a relative error of at most 0.011.
Values may be sent and summed in bfloat16 or wider, within the bound.
A program may use at most 128 MiB of HBM per device.

v0:
```python
import math

import jax
import jax.numpy as jnp
from jax import lax
from jax.sharding import PartitionSpec as P

HEAD_SIZE = 128
QUERY_PER_GROUP = 4


ROPE_BASE = 500000.0


def from_partner(array, axis, apart):
    return lax.ppermute(array, axis, [(i, i ^ 1 << apart) for i in range(lax.axis_size(axis))])


def passed_along(value, axis, steps):
    count = lax.axis_size(axis)
    pairs = [(source, (source + steps) % count) for source in range(count)]
    return lax.ppermute(value, axis, pairs)


def rotary_tables(positions, head_width):
    half_width = head_width // 2
    frequency = jnp.exp(
        jnp.arange(half_width, dtype=jnp.float32) * (-2.0 * math.log(ROPE_BASE) / head_width)
    )
    angles = positions.astype(jnp.float32)[:, None] * frequency[None, :]
    cosine_lookup = jnp.concatenate([jnp.cos(angles), jnp.cos(angles)], axis=1)
    sine_lookup = jnp.concatenate([jnp.sin(angles), jnp.sin(angles)], axis=1)
    return (cosine_lookup, sine_lookup)


def rotate(tensor, cosine_lookup, sine_lookup):
    half_width = tensor.shape[-1] // 2
    turned = jnp.concatenate([-tensor[..., half_width:], tensor[..., :half_width]], axis=-1)
    return tensor * cosine_lookup[:, None, :] + turned * sine_lookup[:, None, :]


def inverse_rotation(gradient, cosine_lookup, sine_lookup):
    half_width = gradient.shape[-1] // 2
    shifted = gradient * sine_lookup[:, None, :]
    turned = jnp.concatenate([shifted[..., half_width:], -shifted[..., :half_width]], axis=-1)
    return gradient * cosine_lookup[:, None, :] + turned


def allowed_pairs(positions):
    offsets = jnp.arange(positions.shape[0], dtype=jnp.int32)
    starts = offsets - positions
    return (offsets[None, :] <= offsets[:, None]) & (starts[:, None] == starts[None, :])


def attend_back(query_rot, key_rot, value_rows, grad_block, allowed):
    score_scale = 1.0 / math.sqrt(query_rot.shape[-1])
    scores = (
        jnp.einsum("qhd,khd->hqk", query_rot, key_rot, preferred_element_type=jnp.float32)
        * score_scale
    )
    scores = jnp.where(allowed[None], scores, -jnp.inf)
    row_peak = jnp.max(scores, axis=-1, keepdims=True)
    weights = jnp.exp(scores - row_peak)
    probability = weights / jnp.sum(weights, axis=-1, keepdims=True)
    prob_rounded = probability.astype(jnp.bfloat16)
    grad_prob = jnp.einsum(
        "qhd,khd->hqk", grad_block, value_rows, preferred_element_type=jnp.float32
    )
    row_delta = jnp.sum(probability * grad_prob, axis=-1, keepdims=True)
    grad_score = (probability * (grad_prob - row_delta) * score_scale).astype(jnp.bfloat16)
    grad_query = jnp.einsum("hqk,khd->qhd", grad_score, key_rot, preferred_element_type=jnp.float32)
    key_gradient = jnp.einsum(
        "hqk,qhd->khd", grad_score, query_rot, preferred_element_type=jnp.float32
    )
    value_gradient = jnp.einsum(
        "hqk,qhd->khd", prob_rounded, grad_block, preferred_element_type=jnp.float32
    )
    return (grad_query, key_gradient, value_gradient)


def on_device(inputs, context_gradient, positions, query_weight, key_value_weight):
    tok_rows = inputs.shape[0]
    block_rows = query_weight.shape[0]
    query_cols = query_weight.shape[1]
    local_heads = query_cols // HEAD_SIZE
    local_groups = key_value_weight.shape[2] // HEAD_SIZE
    pair_index = lax.axis_index("sub")
    weight_cols = jnp.concatenate([query_weight, key_value_weight.reshape(block_rows, -1)], axis=1)
    columns = inputs
    projection = jnp.dot(
        columns,
        lax.all_gather(weight_cols, "blk", axis=0, tiled=True),
        preferred_element_type=jnp.float32,
    )
    projection = projection.astype(jnp.bfloat16)
    query_rows = projection[:, :query_cols].reshape(tok_rows, local_heads, HEAD_SIZE)
    own_proj = projection[:, query_cols:]
    peer_proj = from_partner(own_proj, "sub", 0)
    key_rows = jnp.where(pair_index == 0, own_proj, peer_proj).reshape(
        tok_rows, local_groups, HEAD_SIZE
    )
    value_rows = jnp.where(pair_index == 0, peer_proj, own_proj).reshape(
        tok_rows, local_groups, HEAD_SIZE
    )
    cosine_lookup, sine_lookup = rotary_tables(positions, HEAD_SIZE)
    query_rot = rotate(query_rows.astype(jnp.float32), cosine_lookup, sine_lookup).astype(
        jnp.bfloat16
    )
    key_rot = rotate(key_rows.astype(jnp.float32), cosine_lookup, sine_lookup).astype(jnp.bfloat16)
    head_group = (
        pair_index * local_heads + jnp.arange(local_heads, dtype=jnp.int32)
    ) // QUERY_PER_GROUP
    group_pick = (head_group[:, None] == jnp.arange(local_groups, dtype=jnp.int32)[None, :]).astype(
        jnp.bfloat16
    )
    key_full = jnp.einsum(
        "kgd,hg->khd", key_rot, group_pick, preferred_element_type=jnp.float32
    ).astype(jnp.bfloat16)
    value_full = jnp.einsum(
        "kgd,hg->khd", value_rows, group_pick, preferred_element_type=jnp.float32
    ).astype(jnp.bfloat16)
    grad_query, key_gradient, value_gradient = attend_back(
        query_rot,
        key_full,
        value_full,
        context_gradient.reshape(tok_rows, local_heads, HEAD_SIZE),
        allowed_pairs(positions),
    )
    query_gradient_rows = (
        inverse_rotation(grad_query, cosine_lookup, sine_lookup)
        .astype(jnp.bfloat16)
        .reshape(tok_rows, query_cols)
    )
    pick_float = group_pick.astype(jnp.float32)
    key_part = inverse_rotation(
        jnp.einsum("khd,hg->kgd", key_gradient, pick_float, precision=lax.Precision.HIGHEST),
        cosine_lookup,
        sine_lookup,
    )
    value_part = jnp.einsum(
        "khd,hg->kgd", value_gradient, pick_float, precision=lax.Precision.HIGHEST
    )
    key_sum, value_sum = lax.psum((key_part, value_part), "sub")
    own_grads = (
        jnp.where(pair_index == 0, key_sum, value_sum).astype(jnp.bfloat16).reshape(tok_rows, -1)
    )
    grad_proj = jnp.concatenate([query_gradient_rows, own_grads], axis=1)
    partial_inputs = lax.dot_general(
        grad_proj,
        lax.all_gather(weight_cols, "blk", axis=0, tiled=True),
        (((1,), (1,)), ((), ())),
        preferred_element_type=jnp.float32,
    )
    grad_inputs = lax.psum_scatter(
        partial_inputs, ("tp", "sub"), scatter_dimension=1, tiled=True
    ).astype(jnp.bfloat16)
    shards = lax.axis_size("blk")
    cycle_index = lax.axis_index("blk")
    step_by = 1

    def block_term(turn_index):
        block_index = jnp.mod(cycle_index - step_by * (turn_index + 1), shards)
        columns = lax.dynamic_slice_in_dim(inputs, block_index * block_rows, block_rows, 1)
        return lax.dot_general(
            columns, grad_proj, (((0,), (0,)), ((), ())), preferred_element_type=jnp.float32
        )

    def pass_along(turn_index, gradient_sum):
        return passed_along(gradient_sum, "blk", step_by) + block_term(turn_index)

    gradient_sum = lax.fori_loop(1, shards, pass_along, block_term(0))
    grad_query_out = gradient_sum[:, :query_cols].astype(jnp.bfloat16)
    grad_keyval_out = gradient_sum[:, query_cols:].reshape(block_rows, 1, -1).astype(jnp.bfloat16)
    return (grad_inputs, grad_query_out, grad_keyval_out)


def solution(mesh):
    in_specs = (
        P(("parts", "blk"), None),
        P(("parts", "blk"), ("tp", "sub")),
        P(("parts", "blk")),
        P("blk", ("tp", "sub")),
        P("blk", "sub", "tp"),
    )
    out_specs = (
        P(("parts", "blk"), ("tp", "sub")),
        P(("parts", "blk"), ("tp", "sub")),
        P(("parts", "blk"), "sub", "tp"),
    )
    return jax.shard_map(
        on_device, mesh=mesh, in_specs=in_specs, out_specs=out_specs, check_vma=False
    )
```

profile of v0, /device:TPU:2, one launch (start us, length us, event | category | flops | bytes accessed | tf_op | source)
XLA Modules:
  0.0 755.4 jit_solution(12351098019153917072)
XLA Ops:
  7.2 3.8 pad_maximum_fusion
  11.1 0.6 copy-done.9
  11.7 0.3 multiply_cosine_fusion
  12.3 0.7 fusion.38
  13.0 217.6 %all-gather.2.cloned.1.call-done = bf16[4096,1536]{1,0:T(8,128)(2,1)} async-done(((bf16[1024,1536]{1,0:T(8,128)(2,1)}), bf16[4096,1536]{1,0:T(8,128)(2,1)}) %all-gather.2.cloned.1.call-update) | async-done | bytes 12582928 | tf_op jit(solution)/shard_map/all_gather | solution.py:92
  230.7 6.6 fusion.4
  237.4 0.1 collective-permute-start.1
  237.7 1.0 fusion.11
  238.6 0.4 collective-permute-done.1
  239.0 0.7 broadcast_select_fusion.1
  239.8 0.9 copy.22
  240.7 1.1 copy.9
  241.8 0.3 slice_negate_fusion.3
  242.1 0.6 copy-done.8
  242.7 1.1 fusion.52
  243.9 1.5 fusion.9
  245.4 1.3 copy.16
  246.7 2.8 fusion.25
  249.6 3.2 fusion.58
  252.8 3.0 fusion.17
  255.8 5.4 fusion.21
  261.2 5.5 broadcast_multiply_fusion
  266.7 2.5 copy.25
  269.2 1.8 fusion.14
  271.1 0.1 multiply_bitcast_fusion
  271.2 0.4 fusion.57
  271.6 0.4 maximum_add_fusion.1
  272.0 0.4 copy-done.7
  272.4 1.2 convolution_bitcast_fusion.1
  273.6 6.8 all-reduce.2
  280.5 1.4 fusion.56
  281.9 0.1 copy-done.6
  282.0 0.2 fusion.12
  282.2 0.2 copy.20
  282.4 14.1 %fusion.55 = f32[256,4096]{1,0:T(8,128)} fusion(bf16[4096,1536]{1,0:T(8,128)(2,1)} %all-gather.2.cloned.1.call-done, bf16[256,512]{1,0:T(8,128)(2,1)S(1)} %bitcast.92, bf16[256,1024]{1,0:T(8,128)(2,1)S(1)} %copy.20), kind=kOutput, calls=%fused_computation.88 | convolution fusion | flops 3222798336 | bytes 17563648 | tf_op jit(solution)/shard_map/dot_general | solution.py:148
  296.6 1.0 pad_maximum_fusion.1
  297.6 4.8 fusion.31
  302.4 438.2 %while.17 = (s32[]{:T(128)}, f32[1024,1536]{1,0:T(8,128)}, s32[]{:T(128)}, bf16[256,4096]{1,0:T(8,128)(2,1)S(1)}, bf16[256,1536]{1,0:T(8,128)(2,1)S(1)}, /*index...) while((s32[]{:T(128)}, f32[1024,1536]{1,0:T(8,128)}, ...), condition=%wide.region_7.8_spmd, body=%wide.region_6.7_spmd.sunk | while | flops 806879232 | bytes 39059788 | solution.py:171
  302.4 140.0 %collective-permute-done = f32[1024,1536]{1,0:T(8,128)} collective-permute-done((f32[1024,1536]{1,0:T(8,128)}, f32[1024,1536]{1,0:T(8,128)}, u32[]{:S(2)}, u32[]{:S(2)}) %collective-permute-start) | collective-permute-done | bytes 6291488 | tf_op jit(solution)/shard_map/while/body/eval_jaxpr/ppermute | solution.py:22
  442.4 6.5 convolution_add_fusion.2
  448.9 139.8 %collective-permute-done = f32[1024,1536]{1,0:T(8,128)} collective-permute-done((f32[1024,1536]{1,0:T(8,128)}, f32[1024,1536]{1,0:T(8,128)}, u32[]{:S(2)}, u32[]{:S(2)}) %collective-permute-start) | collective-permute-done | bytes 6291488 | tf_op jit(solution)/shard_map/while/body/eval_jaxpr/ppermute | solution.py:22
  588.7 6.5 convolution_add_fusion.2
  595.2 139.0 %collective-permute-done = f32[1024,1536]{1,0:T(8,128)} collective-permute-done((f32[1024,1536]{1,0:T(8,128)}, f32[1024,1536]{1,0:T(8,128)}, u32[]{:S(2)}, u32[]{:S(2)}) %collective-permute-start) | collective-permute-done | bytes 6291488 | tf_op jit(solution)/shard_map/while/body/eval_jaxpr/ppermute | solution.py:22
  734.2 6.5 convolution_add_fusion.2
  740.6 3.2 convert.6
  743.8 1.6 slice.60
  745.5 1.0 slice_bitcast_fusion
  746.5 2.1 convert_element_type.78
  (37 shorter events, 0.7 us)
Async XLA Ops:
  7.2 239.6 %copy-start = (bf16[256,1024]{1,0:T(8,128)(2,1)S(1)}, bf16[256,1024]{1,0:T(8,128)(2,1)}, u32[]{:S(2)}) copy-start(bf16[256,1024]{1,0:T(8,128)(2,1)} %param.8) | copy-start | bytes 1572868
  7.2 223.5 %all-gather.2.cloned.1.call-start = ((), (), s32[]{:S(2)}) async-start(), calls=%async_computation.1 | async-start | bytes 15728640 | tf_op jit(solution)/shard_map/all_gather | solution.py:92
  11.0 0.7 copy-start.9
  11.0 219.6 %copy-start.2 = (bf16[256,4096]{1,0:T(8,128)(2,1)S(1)}, bf16[256,4096]{1,0:T(8,128)(2,1)}, u32[]{:S(2)}) copy-start(bf16[256,4096]{1,0:T(8,128)(2,1)} %param.7) | copy-start | bytes 6291460
  11.1 735.4 %reduce-scatter.2.cloned.1.call-start = ((), (), s32[]{:S(2)}) async-start(), calls=%async_computation.2 | async-start | bytes 5242880 | tf_op jit(solution)/shard_map/reduce_scatter | solution.py:154
  12.1 225.6 %copy-start.4 = (f32[256,128]{0,1:T(8,128)}, f32[256,128]{0,1:T(8,128)S(1)}, u32[]{:S(2)}) copy-start(f32[256,128]{0,1:T(8,128)S(1)} %get-tuple-element.204) | copy-start | bytes 393220
  237.4 1.6 collective-permute-start.1
  241.8 1.0 copy-start.8
  255.8 5.4 copy-start.5
  271.2 1.2 copy-start.7
  280.4 1.6 copy-start.6
  280.5 2.0 copy-start.3
  302.4 140.0 %collective-permute-start = (f32[1024,1536]{1,0:T(8,128)}, f32[1024,1536]{1,0:T(8,128)}, u32[]{:S(2)}, u32[]{:S(2)}) collective-permute-start(f32[1024,1536]{1,0:T(8,128)} %get-tuple-element.249), channel_id=1, source_target_pairs={{0,4},{4,8},{8,12},{12,0},{1,5},{5,9},{9,13},{13,1},{2,6},{6,10},{... | collective-permute-start | bytes 18874376 | tf_op jit(solution)/shard_map/while/body/eval_jaxpr/ppermute | solution.py:22
  448.9 139.8 %collective-permute-start = (f32[1024,1536]{1,0:T(8,128)}, f32[1024,1536]{1,0:T(8,128)}, u32[]{:S(2)}, u32[]{:S(2)}) collective-permute-start(f32[1024,1536]{1,0:T(8,128)} %get-tuple-element.249), channel_id=1, source_target_pairs={{0,4},{4,8},{8,12},{12,0},{1,5},{5,9},{9,13},{13,1},{2,6},{6,10},{... | collective-permute-start | bytes 18874376 | tf_op jit(solution)/shard_map/while/body/eval_jaxpr/ppermute | solution.py:22
  595.2 139.0 %collective-permute-start = (f32[1024,1536]{1,0:T(8,128)}, f32[1024,1536]{1,0:T(8,128)}, u32[]{:S(2)}, u32[]{:S(2)}) collective-permute-start(f32[1024,1536]{1,0:T(8,128)} %get-tuple-element.249), channel_id=1, source_target_pairs={{0,4},{4,8},{8,12},{12,0},{1,5},{5,9},{9,13},{13,1},{2,6},{6,10},{... | collective-permute-start | bytes 18874376 | tf_op jit(solution)/shard_map/while/body/eval_jaxpr/ppermute | solution.py:22
  743.8 4.8 copy-start.1
Sparse Core Ops, SparseCore 0:
  11.2 219.4 all-gather.1
  296.7 42.4 reduce-scatter.1
where the time goes:
time: 758 us; the launch traced here: 755 us
  waiting for transfers between devices  637 us (84%)
  matrix products  70.5 us (9%)
  other arithmetic  15.9 us (2%)
  between operations  14.3 us (2%)
  local copies, waits for them, and re-layouts  10.8 us (1%)
    ppermute x3, waiting for transfers between devices, passed_along(): return lax.ppermute(value, axis, pairs)  419 us
    all_gather x1, waiting for transfers between devices, on_device(): lax.all_gather(weight_cols, 'blk', axis=0, tiled=True)  218 us
    dot_general x4, matrix products, block_term(): lax.dot_general(columns, grad_proj, (((0,), (0,)), ((), ())), preferred_e...  24.1 us
  transfers between devices with their start and end apart: 6, of which 5 were waited for; matrix products, arithmetic and copies ran while one was open for 4% of the time, Pallas kernels for 0%

commit v1 on v0

--- a/solution.py
+++ b/solution.py
@@ -78,6 +78,29 @@
     return (grad_query, key_gradient, value_gradient)
 
 
+def ring_sum(term, axis):
+    count = lax.axis_size(axis)
+    here = lax.axis_index(axis)
+    total = None
+    for step in range(count):
+        block = term(jnp.mod(here - step - 1, count))
+        if total is not None:
+            block = block + passed_along(total, axis, 1).astype(jnp.float32)
+        total = block.astype(jnp.bfloat16)
+    return total
+
+
+def ring_gather(value, axis):
+    count = lax.axis_size(axis)
+    here = lax.axis_index(axis)
+    whole = jnp.zeros((count,) + value.shape, value.dtype)
+    for step in range(count):
+        whole = lax.dynamic_update_index_in_dim(whole, value, jnp.mod(here - step, count), 0)
+        if step + 1 < count:
+            value = passed_along(value, axis, 1)
+    return whole
+
+
 def on_device(inputs, context_gradient, positions, query_weight, key_value_weight):
     tok_rows = inputs.shape[0]
     block_rows = query_weight.shape[0]
@@ -85,14 +108,22 @@
     local_heads = query_cols // HEAD_SIZE
     local_groups = key_value_weight.shape[2] // HEAD_SIZE
     pair_index = lax.axis_index("sub")
+    blocks = lax.axis_size("blk")
+    sharers = lax.axis_size("tp") * lax.axis_size("sub")
+    share = lax.axis_index("tp") * lax.axis_size("sub") + pair_index
     weight_cols = jnp.concatenate([query_weight, key_value_weight.reshape(block_rows, -1)], axis=1)
-    columns = inputs
-    projection = jnp.dot(
-        columns,
-        lax.all_gather(weight_cols, "blk", axis=0, tiled=True),
-        preferred_element_type=jnp.float32,
-    )
-    projection = projection.astype(jnp.bfloat16)
+    share_rows = tok_rows // sharers
+    shared = lax.dynamic_slice_in_dim(inputs, share * share_rows, share_rows, 0)
+    shared = lax.all_to_all(
+        shared.reshape(share_rows, blocks, block_rows).transpose(1, 0, 2), "blk", 0, 0, tiled=True
+    )
+    columns = lax.all_gather(shared, ("tp", "sub"), axis=1, tiled=True)
+
+    def projection_term(block):
+        rows = lax.dynamic_index_in_dim(columns, block, 0, keepdims=False)
+        return jnp.dot(rows, weight_cols, preferred_element_type=jnp.float32)
+
+    projection = ring_sum(projection_term, "blk")
     query_rows = projection[:, :query_cols].reshape(tok_rows, local_heads, HEAD_SIZE)
     own_proj = projection[:, query_cols:]
     peer_proj = from_partner(own_proj, "sub", 0)
@@ -140,37 +171,31 @@
     value_part = jnp.einsum(
         "khd,hg->kgd", value_gradient, pick_float, precision=lax.Precision.HIGHEST
     )
-    key_sum, value_sum = lax.psum((key_part, value_part), "sub")
-    own_grads = (
-        jnp.where(pair_index == 0, key_sum, value_sum).astype(jnp.bfloat16).reshape(tok_rows, -1)
-    )
+    mine = jnp.where(pair_index == 0, key_part, value_part)
+    other = jnp.where(pair_index == 0, value_part, key_part)
+    own_grads = (mine + from_partner(other, "sub", 0)).astype(jnp.bfloat16).reshape(tok_rows, -1)
     grad_proj = jnp.concatenate([query_gradient_rows, own_grads], axis=1)
+
+    all_grads = ring_gather(grad_proj, "blk").reshape(blocks * tok_rows, -1)
+    gradient_sum = lax.dot_general(
+        columns.reshape(blocks * tok_rows, block_rows),
+        all_grads,
+        (((0,), (0,)), ((), ())),
+        preferred_element_type=jnp.float32,
+    ).astype(jnp.bfloat16)
     partial_inputs = lax.dot_general(
-        grad_proj,
-        lax.all_gather(weight_cols, "blk", axis=0, tiled=True),
-        (((1,), (1,)), ((), ())),
-        preferred_element_type=jnp.float32,
-    )
-    grad_inputs = lax.psum_scatter(
-        partial_inputs, ("tp", "sub"), scatter_dimension=1, tiled=True
-    ).astype(jnp.bfloat16)
-    shards = lax.axis_size("blk")
-    cycle_index = lax.axis_index("blk")
-    step_by = 1
-
-    def block_term(turn_index):
-        block_index = jnp.mod(cycle_index - step_by * (turn_index + 1), shards)
-        columns = lax.dynamic_slice_in_dim(inputs, block_index * block_rows, block_rows, 1)
-        return lax.dot_general(
-            columns, grad_proj, (((0,), (0,)), ((), ())), preferred_element_type=jnp.float32
-        )
-
-    def pass_along(turn_index, gradient_sum):
-        return passed_along(gradient_sum, "blk", step_by) + block_term(turn_index)
-
-    gradient_sum = lax.fori_loop(1, shards, pass_along, block_term(0))
-    grad_query_out = gradient_sum[:, :query_cols].astype(jnp.bfloat16)
-    grad_keyval_out = gradient_sum[:, query_cols:].reshape(block_rows, 1, -1).astype(jnp.bfloat16)
+        all_grads, weight_cols, (((1,), (1,)), ((), ())), preferred_element_type=jnp.float32
+    ).astype(jnp.bfloat16)
+    pieces = lax.all_to_all(
+        partial_inputs.reshape(sharers, -1, block_rows), ("tp", "sub"), 0, 0, tiled=True
+    )
+    grad_inputs = jnp.sum(pieces.astype(jnp.float32), axis=0).astype(jnp.bfloat16)
+    swaps = [
+        (b * sharers + s, s * sharers + b) for b in range(blocks) for s in range(sharers)
+    ]
+    grad_inputs = lax.ppermute(grad_inputs, ("blk", "tp", "sub"), swaps)
+    grad_query_out = gradient_sum[:, :query_cols]
+    grad_keyval_out = gradient_sum[:, query_cols:].reshape(block_rows, 1, -1)
     return (grad_inputs, grad_query_out, grad_keyval_out)
 
 

time: 758 us -> 295 us (0.39)
  waiting for transfers between devices: 637 us -> 151 us
  blocking collectives: 6.78 us -> 48.1 us
  matrix products: 70.5 us -> 47.7 us
    ppermute x3 -> x6, waiting for transfers between devices: 419 us -> 114 us  [passed_along(): return lax.ppermute(value, axis, pairs)]
    all_gather x1, waiting for transfers between devices: 218 us -> 20.7 us  [on_device(): columns = lax.all_gather(shared, ('tp', 'sub'), axis=1, tiled=True)]
    all_to_all x0 -> x2, blocking collectives: none -> 48.1 us  [the longest x1 28.9 us: on_device(): lax.all_to_all(partial_inputs.reshape(sharers, -1, block_rows), ('tp', 's...]
    dot_general x6, matrix products: 44.9 us -> 23.4 us  [the longest x4 13.7 us: projection_term(): return jnp.dot(rows, weight_cols, preferred_element_type=jnp.float32)]
    ppermute x0 -> x1, waiting for transfers between devices: none -> 15.6 us  [on_device(): grad_inputs = lax.ppermute(grad_inputs, ('blk', 'tp', 'sub'), swaps)]
  transfers between devices with their start and end apart: 6 -> 10, of which waited for: 5 -> 8; matrix products, arithmetic and copies ran while one was open for 4% -> 8% of each run, Pallas kernels for 0% -> 0%
where the time goes in v1:
time: 295 us; the launch traced here: 294 us
  waiting for transfers between devices  151 us (51%)
  blocking collectives  48.1 us (16%)
  matrix products  47.7 us (16%)
  local copies, waits for them, and re-layouts  17.1 us (6%)
  between operations  14.5 us (5%)
  other arithmetic  11.6 us (4%)
  starting transfers between devices  4.27 us (1%)
    ppermute x6, waiting for transfers between devices, passed_along(): return lax.ppermute(value, axis, pairs)  114 us
    all_to_all x1, blocking collectives, on_device(): lax.all_to_all(partial_inputs.reshape(sharers, -1, block_rows), ('tp', 's...  28.9 us
    all_gather x1, waiting for transfers between devices, on_device(): columns = lax.all_gather(shared, ('tp', 'sub'), axis=1, tiled=True)  20.7 us
    all_to_all x1, blocking collectives, on_device(): lax.all_to_all(shared.reshape(share_rows, blocks, block_rows).transpose(1...  19.3 us
    ppermute x1, waiting for transfers between devices, on_device(): grad_inputs = lax.ppermute(grad_inputs, ('blk', 'tp', 'sub'), swaps)  15.6 us
    dot_general x4, matrix products, projection_term(): return jnp.dot(rows, weight_cols, preferred_element_type=jnp.float32)  13.7 us
    dot_general x1, matrix products, on_device(): lax.dot_general(columns.reshape(blocks * tok_rows, block_rows), all_grads...  5.99 us
  transfers between devices with their start and end apart: 10, of which 8 were waited for; matrix products, arithmetic and copies ran while one was open for 8% of the time, Pallas kernels for 0%

profile of v1, /device:TPU:2, one launch (start us, length us, event | category | flops | bytes accessed | tf_op | source)
XLA Modules:
  0.0 293.9 jit_solution(13629115645331183462)
XLA Ops:
  7.2 1.5 copy-done
  8.8 19.3 %all_to_all.10 = bf16[4,64,1024]{2,1,0:T(8,128)(2,1)} all-to-all(bf16[4,64,1024]{2,1,0:T(8,128)(2,1)S(1)} %bitcast.122), channel_id=1, replica_groups=mesh['parts'=2,'blk'=4,'tp'=2,'sub'=2] {'blk'}, dimensions={0} | all-to-all | bytes 1048576 | tf_op jit(solution)/shard_map/all_to_all | solution.py:117
  28.2 20.7 %all-gather.2.cloned.1.call-done = bf16[4,256,1024]{2,1,0:T(8,128)(2,1)} async-done(((bf16[4,64,1024]{2,1,0:T(8,128)(2,1)}), bf16[4,256,1024]{2,1,0:T(8,128)(2,1)}) %all-gather.2.cloned.1.call-update) | async-done | bytes 2097168 | tf_op jit(solution)/shard_map/all_gather | solution.py:120
  48.8 3.6 %convolution_convert_fusion = bf16[256,1536]{1,0:T(8,128)(2,1)} fusion(bf16[4,256,1024]{2,1,0:T(8,128)(2,1)} %all-gather.2.cloned.1.call-done, s32[]{:T(128)S(6)} %select_n.99, bf16[1024,512]{1,0:T(8,128)(2,1)S(1)} %bitcast.128, bf16[1024,1024]{1,0:T(8,128)(2,1)} %param.8), kind=kOutput, calls=%fused_computation.4 | convolution fusion | flops 811991040 | bytes 4456452 | tf_op jit(solution)/shard_map/dot_general | solution.py:124
  52.4 1.7 collective-permute-start
  54.2 20.0 %collective-permute-done = bf16[256,1536]{1,0:T(8,128)(2,1)S(1)} collective-permute-done((bf16[256,1536]{1,0:T(8,128)(2,1)}, bf16[256,1536]{1,0:T(8,128)(2,1)S(1)}, u32[]{:S(2)}, u32[]{:S(2)}) %collective-permute-start) | collective-permute-done | bytes 786464 | tf_op jit(solution)/shard_map/ppermute | solution.py:22
  74.2 3.9 %add_convert_fusion.2 = bf16[256,1536]{1,0:T(8,128)(2,1)} fusion(bf16[256,1536]{1,0:T(8,128)(2,1)S(1)} %collective-permute-done, bf16[4,256,1024]{2,1,0:T(8,128)(2,1)} %all-gather.2.cloned.1.call-done, s32[]{:T(128)S(6)} %select_n.97, bf16[1024,512]{1,0:T(8,128)(2,1)} %bitcast.125, bf16[1024,1024]{1,0:T(8,128)(2,1)} %param.8), kind=kOutput, calls=%fused_computation.16 | convolution fusion | flops 812777472 | bytes 5242884 | tf_op jit(solution)/shard_map/dot_general | solution.py:124
  78.1 3.1 %fusion.33 = f32[256,1536]{1,0:T(8,128)S(1)} fusion(bf16[4,256,1024]{2,1,0:T(8,128)(2,1)} %all-gather.2.cloned.1.call-done, s32[]{:T(128)S(6)} %select_n.95, bf16[1024,512]{1,0:T(8,128)(2,1)} %bitcast.126, bf16[1024,1024]{1,0:T(8,128)(2,1)} %param.8), kind=kOutput, calls=%fused_computation.62 | convolution fusion | flops 811597824 | bytes 5242884 | tf_op jit(solution)/shard_map/dot_general | solution.py:124
  81.2 17.8 %collective-permute-done.1 = bf16[256,1536]{1,0:T(8,128)(2,1)S(1)} collective-permute-done((bf16[256,1536]{1,0:T(8,128)(2,1)}, bf16[256,1536]{1,0:T(8,128)(2,1)S(1)}, u32[]{:S(2)}, u32[]{:S(2)}) %collective-permute-start.1) | collective-permute-done | bytes 786464 | tf_op jit(solution)/shard_map/ppermute | solution.py:22
  99.0 1.1 add_convert_fusion.1
  100.7 0.7 fusion.46
  101.4 3.1 %fusion.35 = f32[256,1536]{1,0:T(8,128)S(1)} fusion(bf16[4,256,1024]{2,1,0:T(8,128)(2,1)} %all-gather.2.cloned.1.call-done, s32[]{:T(128)S(6)} %select_n.93, bf16[1024,512]{1,0:T(8,128)(2,1)} %bitcast.127, bf16[1024,1024]{1,0:T(8,128)(2,1)} %param.8), kind=kOutput, calls=%fused_computation.64 | convolution fusion | flops 811597824 | bytes 5242884 | tf_op jit(solution)/shard_map/dot_general | solution.py:124
  104.5 15.6 %collective-permute-done.2 = bf16[256,1536]{1,0:T(8,128)(2,1)S(1)} collective-permute-done((bf16[256,1536]{1,0:T(8,128)(2,1)}, bf16[256,1536]{1,0:T(8,128)(2,1)S(1)}, u32[]{:S(2)}, u32[]{:S(2)}) %collective-permute-start.2) | collective-permute-done | bytes 786464 | tf_op jit(solution)/shard_map/ppermute | solution.py:22
  120.3 0.8 slice.48
  121.1 1.1 slice_convert_fusion
  122.2 1.6 copy.40
  123.9 0.8 copy-done.4
  124.7 1.0 fusion.8
  125.7 1.8 broadcast_select_fusion.1
  128.0 0.7 fusion.6
  128.7 1.1 copy.30
  129.8 1.0 reshape.112
  131.2 2.8 fusion.22
  134.1 3.2 %fusion.69 = (f32[8,256]{1,0:T(8,128)S(1)}, f32[8,256,256]{1,2,0:T(8,128)}) fusion(pred[256,256]{0,1:T(8,128)(4,1)S(1)} %copy-done.10, bf16[256,8,128]{0,2,1:T(8,128)(2,1)S(1)} %copy-done.9, bf16[256,8,128]{0,2,1:T(8,128)(2,1)} %fusion.8), kind=kOutput, calls=%fused_computation.112 | convolution fusion | flops 136315136 | bytes 3219456 | tf_op jit(solution)/shard_map/sub | solution.py:63
  137.3 3.1 %fusion.14 = f32[8,256,128]{2,1,0:T(8,128)} fusion(f32[8,256,256]{1,2,0:T(8,128)} %get-tuple-element.20, f32[8,256]{1,0:T(8,128)S(1)} %get-tuple-element.19, bf16[256,1024]{1,0:T(8,128)(2,1)} %param.6), kind=kOutput, calls=%fused_computation.32 | convolution fusion | flops 135266304 | bytes 3678208 | tf_op jit(solution)/shard_map/hqk,qhd->khd/dot_general | solution.py:75
  140.4 5.6 %broadcast_multiply_fusion = (f32[256,8,128]{0,2,1:T(8,128)}, f32[256,8,128]{0,2,1:T(8,128)}) fusion(f32[256,128]{0,1:T(8,128)S(1)} %copy-done.5, bf16[256,8,128]{0,2,1:T(8,128)(2,1)S(1)} %copy-done.9, f32[8,256,256]{2,1,0:T(8,128)} %fusion.22, f32[8,256,256]{1,2,0:T(8,128)} %get-tuple-element.20, f32[8,256]{1,0:T(8,128)S(1)} %get-tuple-element.19), kind=kOutput, calls=%fused_computation.68 | convolution fusion | flops 138152192 | bytes 6955008 | tf_op jit(solution)/shard_map/hqk,khd->qhd/dot_general | solution.py:71
  146.0 5.3 %fusion.18 = f32[8,128,256]{2,1,0:T(8,128)} fusion(bf16[256,8,128]{0,2,1:T(8,128)(2,1)} %fusion.8, f32[8,256,256]{2,1,0:T(8,128)} %fusion.22, f32[8,256,256]{1,2,0:T(8,128)} %get-tuple-element.20, f32[8,256]{1,0:T(8,128)S(1)} %get-tuple-element.19), kind=kOutput, calls=%fused_computation.37 | convolution fusion | flops 137890048 | bytes 5775360 | tf_op jit(solution)/shard_map/hqk,qhd->khd/dot_general | solution.py:72
  151.3 1.6 copy.38
  153.0 0.6 fusion.11
  154.2 2.6 broadcast_select_fusion
  157.4 0.6 copy-done.7
  158.0 1.0 fusion.9
  159.0 1.2 copy.34
  160.2 1.2 add_convert_fusion.3
  161.6 22.0 %collective-permute-done.5 = bf16[256,1536]{1,0:T(8,128)(2,1)} collective-permute-done((bf16[256,1536]{1,0:T(8,128)(2,1)S(1)}, bf16[256,1536]{1,0:T(8,128)(2,1)}, u32[]{:S(2)}, u32[]{:S(2)}) %collective-permute-start.5) | collective-permute-done | bytes 786464 | tf_op jit(solution)/shard_map/ppermute | solution.py:22
  184.0 21.0 %collective-permute-done.6 = bf16[256,1536]{1,0:T(8,128)(2,1)} collective-permute-done((bf16[256,1536]{1,0:T(8,128)(2,1)}, bf16[256,1536]{1,0:T(8,128)(2,1)}, u32[]{:S(2)}, u32[]{:S(2)}) %collective-permute-start.6) | collective-permute-done | bytes 786464 | tf_op jit(solution)/shard_map/ppermute | solution.py:22
  205.0 1.2 bitcast_dynamic-update-slice_fusion.2
  206.2 1.2 bitcast_dynamic-update-slice_fusion.1
  207.4 18.0 %collective-permute-done.7 = bf16[256,1536]{1,0:T(8,128)(2,1)S(1)} collective-permute-done((bf16[256,1536]{1,0:T(8,128)(2,1)}, bf16[256,1536]{1,0:T(8,128)(2,1)S(1)}, u32[]{:S(2)}, u32[]{:S(2)}) %collective-permute-start.7) | collective-permute-done | bytes 786464 | tf_op jit(solution)/shard_map/ppermute | solution.py:22
  225.5 3.7 %convolution_convert_fusion.1 = bf16[1024,1024]{1,0:T(8,128)(2,1)S(1)} fusion(bf16[1024,1536]{1,0:T(8,128)(2,1)S(1)} %bitcast.117, bf16[1024,512]{1,0:T(8,128)(2,1)S(1)} %bitcast.129, bf16[1024,1024]{1,0:T(8,128)(2,1)S(1)} %copy-done.12), kind=kOutput, calls=%fused_computation.12 | convolution fusion | flops 3228565504 | bytes 8388608 | tf_op jit(solution)/shard_map/dot_general | solution.py:186
  229.2 28.9 %all_to_all.11 = bf16[4,256,1024]{2,1,0:T(8,128)(2,1)} all-to-all(bf16[4,256,1024]{2,1,0:T(8,128)(2,1)S(1)} %bitcast.120), channel_id=1, replica_groups=mesh['parts'=2,'blk'=4,'tp'=2,'sub'=2] {'tp','sub'}, dimensions={0} | all-to-all | bytes 4194304 | tf_op jit(solution)/shard_map/all_to_all | solution.py:189
  258.1 2.0 reduce_sum.32
  260.1 1.9 collective-permute-start.8
  262.0 6.0 %bitcast_convert_fusion = bf16[1024,1536]{1,0:T(8,128)(2,1)S(1)} fusion(bf16[4,256,1024]{2,1,0:T(8,128)(2,1)} %all-gather.2.cloned.1.call-done, bf16[4,256,1536]{2,1,0:T(8,128)(2,1)} %copy-done.2), kind=kOutput, calls=%fused_computation.2 | convolution fusion | flops 3222798336 | bytes 8388608 | tf_op jit(solution)/shard_map/dot_general | solution.py:180
  268.0 1.6 slice.58
  269.7 1.0 slice_bitcast_fusion
  270.7 15.6 %collective-permute-done.8 = bf16[256,1024]{1,0:T(8,128)(2,1)S(1)} collective-permute-done((bf16[256,1024]{1,0:T(8,128)(2,1)S(1)}, bf16[256,1024]{1,0:T(8,128)(2,1)S(1)}, u32[]{:S(2)}, u32[]{:S(2)}) %collective-permute-start.8) | collective-permute-done | bytes 524320 | tf_op jit(solution)/shard_map/ppermute | solution.py:196
  286.3 0.8 copy.71
  (60 shorter events, 3.6 us)
Async XLA Ops:
  7.2 1.6 copy-start
  7.2 41.6 %copy-start.13 = (bf16[1024,1,512]{2,0,1:T(8,128)(2,1)S(1)}, bf16[1024,1,512]{2,0,1:T(8,128)(2,1)}, u32[]{:S(2)}) copy-start(bf16[1024,1,512]{2,0,1:T(8,128)(2,1)} %param.9) | copy-start | bytes 3145732
  7.2 41.6 %all-gather.2.cloned.1.call-start = ((), (), s32[]{:S(2)}) async-start(), calls=%async_computation.2 | async-start | bytes 2621440 | tf_op jit(solution)/shard_map/all_gather | solution.py:120
  52.4 21.7 %collective-permute-start = (bf16[256,1536]{1,0:T(8,128)(2,1)}, bf16[256,1536]{1,0:T(8,128)(2,1)S(1)}, u32[]{:S(2)}, u32[]{:S(2)}) collective-permute-start(bf16[256,1536]{1,0:T(8,128)(2,1)} %convolution_convert_fusion), channel_id=1, source_target_pairs={{0,4},{4,8},{8,12},{12,0},{1,5},{5,9},{9,13},{13,1},{2,6},{6,10},{... | collective-permute-start | bytes 2359304 | tf_op jit(solution)/shard_map/ppermute | solution.py:22
  54.2 24.0 %copy-start.11 = (s32[256]{0:T(256)S(1)}, s32[256]{0:T(256)}, u32[]{:S(2)}) copy-start(s32[256]{0:T(256)} %param.7) | copy-start | bytes 3076
  78.1 20.9 %collective-permute-start.1 = (bf16[256,1536]{1,0:T(8,128)(2,1)}, bf16[256,1536]{1,0:T(8,128)(2,1)S(1)}, u32[]{:S(2)}, u32[]{:S(2)}) collective-permute-start(bf16[256,1536]{1,0:T(8,128)(2,1)} %add_convert_fusion.2), channel_id=1, source_target_pairs={{0,4},{4,8},{8,12},{12,0},{1,5},{5,9},{9,13},{13,1},{2,6},{6,10},{... | collective-permute-start | bytes 2359304 | tf_op jit(solution)/shard_map/ppermute | solution.py:22
  100.1 20.0 %collective-permute-start.2 = (bf16[256,1536]{1,0:T(8,128)(2,1)}, bf16[256,1536]{1,0:T(8,128)(2,1)S(1)}, u32[]{:S(2)}, u32[]{:S(2)}) collective-permute-start(bf16[256,1536]{1,0:T(8,128)(2,1)} %add_convert_fusion.1), channel_id=1, source_target_pairs={{0,4},{4,8},{8,12},{12,0},{1,5},{5,9},{9,13},{13,1},{2,6},{6,10},{... | collective-permute-start | bytes 2359304 | tf_op jit(solution)/shard_map/ppermute | solution.py:22
  100.5 4.0 %copy-start.3 = (f32[256,128]{0,1:T(8,128)}, f32[256,128]{0,1:T(8,128)S(1)}, u32[]{:S(2)}) copy-start(f32[256,128]{0,1:T(8,128)S(1)} %get-tuple-element.25) | copy-start | bytes 393220
  120.3 1.9 copy-start.1
  122.2 3.5 %collective-permute-start.3 = (bf16[256,512]{1,0:T(8,128)(2,1)}, bf16[256,512]{1,0:T(8,128)(2,1)}, u32[]{:S(2)}, u32[]{:S(2)}) collective-permute-start(bf16[256,512]{1,0:T(8,128)(2,1)} %slice.48), channel_id=1, source_target_pairs={{0,1},{1,0},{2,3},{3,2},{4,5},{5,4},{6,7},{7,6},{8,9},{9,8},{10,11... | collective-permute-start | bytes 786440 | tf_op jit(solution)/shard_map/ppermute | solution.py:16
  123.8 0.9 copy-start.4
  130.9 3.2 %copy-start.9 = (bf16[256,8,128]{0,2,1:T(8,128)(2,1)S(1)}, bf16[256,8,128]{0,2,1:T(8,128)(2,1)}, u32[]{:S(2)}) copy-start(bf16[256,8,128]{0,2,1:T(8,128)(2,1)} %copy.30) | copy-start | bytes 1572868
  130.9 3.2 %copy-start.10 = (pred[256,256]{0,1:T(8,128)(4,1)S(1)}, pred[256,256]{0,1:T(8,128)(4,1)}, u32[]{:S(2)}) copy-start(pred[256,256]{0,1:T(8,128)(4,1)} %fusion.46) | copy-start | bytes 196612
  137.3 3.1 %copy-start.5 = (f32[256,128]{0,1:T(8,128)S(1)}, f32[256,128]{0,1:T(8,128)}, u32[]{:S(2)}) copy-start(f32[256,128]{0,1:T(8,128)} %copy-done.3) | copy-start | bytes 393220
  153.0 1.2 copy-start.6
  154.2 3.1 %copy-start.8 = (f32[256,8,128]{0,2,1:T(8,128)S(1)}, f32[256,8,128]{0,2,1:T(8,128)}, u32[]{:S(2)}) copy-start(f32[256,8,128]{0,2,1:T(8,128)} %get-tuple-element.22) | copy-start | bytes 3145732
  156.8 1.2 copy-start.7
  156.8 3.4 %collective-permute-start.4 = (f32[256,4,128]{2,1,0:T(4,128)}, f32[256,4,128]{2,1,0:T(4,128)}, u32[]{:S(2)}, u32[]{:S(2)}) collective-permute-start(f32[256,4,128]{2,1,0:T(4,128)} %get-tuple-element.3), channel_id=1, source_target_pairs={{0,1},{1,0},{2,3},{3,2},{4,5},{5,4},{6,7},{7,6},{8,9},{9,8},{10,11... | collective-permute-start | bytes 1572872 | tf_op jit(solution)/shard_map/ppermute | solution.py:16
  161.6 22.1 %collective-permute-start.5 = (bf16[256,1536]{1,0:T(8,128)(2,1)S(1)}, bf16[256,1536]{1,0:T(8,128)(2,1)}, u32[]{:S(2)}, u32[]{:S(2)}) collective-permute-start(bf16[256,1536]{1,0:T(8,128)(2,1)S(1)} %pad_maximum_fusion.1), channel_id=1, source_target_pairs={{0,4},{4,8},{8,12},{12,0},{1,5},{5,9},{9,13},{13,1},{2,6},{6,10},{... | collective-permute-start | bytes 2359304 | tf_op jit(solution)/shard_map/ppermute | solution.py:22
  183.6 21.4 %collective-permute-start.6 = (bf16[256,1536]{1,0:T(8,128)(2,1)}, bf16[256,1536]{1,0:T(8,128)(2,1)}, u32[]{:S(2)}, u32[]{:S(2)}) collective-permute-start(bf16[256,1536]{1,0:T(8,128)(2,1)} %collective-permute-done.5), channel_id=1, source_target_pairs={{0,4},{4,8},{8,12},{12,0},{1,5},{5,9},{9,13},{13,1},{2,6},{6,10},{... | collective-permute-start | bytes 2359304 | tf_op jit(solution)/shard_map/ppermute | solution.py:22
  184.0 41.5 %copy-start.12 = (bf16[1024,1024]{1,0:T(8,128)(2,1)S(1)}, bf16[1024,1024]{1,0:T(8,128)(2,1)}, u32[]{:S(2)}) copy-start(bf16[1024,1024]{1,0:T(8,128)(2,1)} %param.8) | copy-start | bytes 6291460
  184.0 41.5 %copy-start.14 = (bf16[1024,1,512]{2,0,1:T(8,128)(2,1)S(1)}, bf16[1024,1,512]{2,0,1:T(8,128)(2,1)}, u32[]{:S(2)}) copy-start(bf16[1024,1,512]{2,0,1:T(8,128)(2,1)} %param.9) | copy-start | bytes 3145732
  205.0 20.4 %collective-permute-start.7 = (bf16[256,1536]{1,0:T(8,128)(2,1)}, bf16[256,1536]{1,0:T(8,128)(2,1)S(1)}, u32[]{:S(2)}, u32[]{:S(2)}) collective-permute-start(bf16[256,1536]{1,0:T(8,128)(2,1)} %collective-permute-done.6), channel_id=1, source_target_pairs={{0,4},{4,8},{8,12},{12,0},{1,5},{5,9},{9,13},{13,1},{2,6},{6,10},{... | collective-permute-start | bytes 2359304 | tf_op jit(solution)/shard_map/ppermute | solution.py:22
  225.5 3.7 %copy-start.2 = (bf16[4,256,1536]{2,1,0:T(8,128)(2,1)}, bf16[4,256,1536]{2,1,0:T(8,128)(2,1)S(1)}, u32[]{:S(2)}) copy-start(bf16[4,256,1536]{2,1,0:T(8,128)(2,1)S(1)} %bitcast_dynamic-update-slice_fusion) | copy-start | bytes 9437188
  260.1 26.2 %collective-permute-start.8 = (bf16[256,1024]{1,0:T(8,128)(2,1)S(1)}, bf16[256,1024]{1,0:T(8,128)(2,1)S(1)}, u32[]{:S(2)}, u32[]{:S(2)}) collective-permute-start(bf16[256,1024]{1,0:T(8,128)(2,1)S(1)} %reduce_sum.32), channel_id=1, source_target_pairs={{0,0},{1,4},{2,8},{3,12},{4,1},{5,5},{6,9},{7,13},{8,2},{9,6},{10,... | collective-permute-start | bytes 1572872 | tf_op jit(solution)/shard_map/ppermute | solution.py:196
Sparse Core Ops, SparseCore 0:
  28.3 20.5 all-gather.1

commit v2 on v1

--- a/solution.py
+++ b/solution.py
@@ -3,6 +3,8 @@
 import jax
 import jax.numpy as jnp
 from jax import lax
+from jax.experimental import pallas as pl
+from jax.experimental.pallas import tpu as pltpu
 from jax.sharding import PartitionSpec as P
 
 HEAD_SIZE = 128
@@ -101,12 +103,408 @@
     return whole
 
 
+def fused_kernel(
+    x_ref, grad_ref, start_col, start_row, cos_ref, sin_ref, wq_ref, wkv_ref,
+    dx_ref, dwq_ref, dwkv_ref,
+    w_all, x_all, part, sends, inbox, q_sum, kv_out, kv_in, dkv_out, dkv_in, grads, dx_part,
+    dx_send, dx_in, dx_sum, land,
+    x_s, x_r, fan_s, fan_r, flow_s, flow_r, kv_s, kv_r, dkv_s, dkv_r, ag_s, ag_r, dx_s, dx_r, end_s, end_r,
+):
+    size = HEAD_SIZE
+    half_q = wq_ref.shape[1] // 2
+    width = half_q + 2 * size
+    heads = half_q // size
+    tokens = x_ref.shape[0]
+    depth = wq_ref.shape[0]
+    share_rows = tokens // 4
+    me = lax.axis_index("blk")
+    tp = lax.axis_index("tp")
+    sub = lax.axis_index("sub")
+    share = tp * 2 + sub
+    low = me < 2
+    middle = (me == 1) | (me == 2)
+    outer = jnp.logical_not(middle)
+    order = [jnp.where(low, 3 - j, j) for j in range(4)]
+    ahead = jnp.where(low, me + 1, me - 1)
+    behind = jnp.where(low, jnp.maximum(me - 1, 0), jnp.minimum(me + 1, 3))
+    main = jnp.where(low, 0, 1)
+    others = [order[0], order[1], jnp.where(middle, order[3], order[2])]
+    mates = [lax.rem(share + r, 4) for r in (1, 2, 3)]
+
+    def send(src, dst, send_sem, recv_sem, **where):
+        return pltpu.make_async_remote_copy(
+            src_ref=src, dst_ref=dst, send_sem=send_sem, recv_sem=recv_sem,
+            device_id=where, device_id_type=pl.DeviceIdType.MESH,
+        )
+
+    barrier = pltpu.get_barrier_semaphore()
+    for j in others:
+        pl.semaphore_signal(barrier, inc=1, device_id={"blk": j}, device_id_type=pl.DeviceIdType.MESH)
+    for q in mates:
+        pl.semaphore_signal(
+            barrier, inc=1, device_id={"tp": q // 2, "sub": lax.rem(q, 2)},
+            device_id_type=pl.DeviceIdType.MESH,
+        )
+    crossing = me != share
+
+    @pl.when(crossing)
+    def _():
+        pl.semaphore_signal(
+            barrier, inc=1,
+            device_id={"blk": share, "tp": me // 2, "sub": lax.rem(me, 2)},
+            device_id_type=pl.DeviceIdType.MESH,
+        )
+
+    pl.semaphore_wait(barrier, 6 + jnp.where(crossing, 1, 0))
+
+    my_rows = pl.ds(pl.multiple_of(share * share_rows, share_rows), share_rows)
+
+    def rows_of(q):
+        return pl.ds(pl.multiple_of(q * share_rows, share_rows), share_rows)
+
+    def x_first(j, t):
+        return send(
+            x_ref.at[my_rows, pl.ds(pl.multiple_of(j * depth, depth), depth)],
+            x_all.at[t, my_rows, :], x_s.at[j], x_r.at[t], blk=j,
+        )
+
+    for j in others:
+        x_first(j, me).start()
+
+    x_all[me] = x_ref[:, pl.ds(pl.multiple_of(me * depth, depth), depth)]
+    for h in range(2):
+        w_all[h, :, :half_q] = wq_ref[:, h * half_q : (h + 1) * half_q]
+        w_all[h, :, half_q : half_q + size] = wkv_ref[:, h * size : (h + 1) * size]
+        w_all[h, :, half_q + size :] = wkv_ref[:, (h + 2) * size : (h + 3) * size]
+
+    def fan(t, r, q):
+        return send(
+            x_all.at[t, my_rows, :], x_all.at[t, my_rows, :], fan_s.at[t, r], fan_r.at[t, r],
+            tp=q // 2, sub=lax.rem(q, 2),
+        )
+
+    for t in others:
+        x_first(t, t).wait_recv()
+        for r in range(3):
+            fan(t, r, mates[r]).start()
+
+    def fan_wait(t):
+        for r in range(3):
+            q = lax.rem(share + 3 - r, 4)
+            send(
+                x_all.at[t, rows_of(q), :], x_all.at[t, rows_of(q), :], fan_s.at[t, r],
+                fan_r.at[t, r], tp=q // 2, sub=lax.rem(q, 2),
+            ).wait_recv()
+
+    def flow(h, d, way, to):
+        return send(sends.at[h, d], inbox.at[h, way, d], flow_s.at[h, d], flow_r.at[h, way, d], blk=to)
+
+    tile = 256
+
+    def project(h, d):
+        @pl.loop(0, width // tile)
+        def _(n):
+            cols = pl.ds(pl.multiple_of(n * tile, tile), tile)
+            part[h, d, :, cols] = jnp.dot(
+                x_all[d], w_all[h, :, cols], preferred_element_type=jnp.float32
+            )
+
+    for h in range(2):
+        for j in range(4):
+            d = order[j]
+            if h == 0:
+                @pl.when(d != me)
+                def _():
+                    fan_wait(d)
+            project(h, d)
+            if j < 3:
+                @pl.when(outer)
+                def _():
+                    sends[h, d] = part[h, d].astype(jnp.bfloat16)
+                    flow(h, d, main, ahead).start()
+
+    def pass_on(h, d, way, to):
+        @pl.when(middle)
+        def _():
+            flow(h, d, way, to).wait_recv()
+            sends[h, d] = (part[h, d] + inbox[h, way, d].astype(jnp.float32)).astype(jnp.bfloat16)
+            flow(h, d, way, to).start()
+
+    scale = 1.0 / math.sqrt(size)
+    cos = cos_ref[...]
+    sin = sin_ref[...]
+
+    def turn(u):
+        return u * cos + pltpu.roll(u, size // 2, 1) * sin
+
+    def turn_back(u):
+        return u * cos - pltpu.roll(u, size // 2, 1) * sin
+
+    def attend(h):
+        flow(h, me, 1 - main, ahead).wait_recv()
+        total = part[h, me] + inbox[h, 1 - main, me].astype(jnp.float32)
+        part[h, me] = total
+
+        @pl.when(middle)
+        def _():
+            flow(h, me, main, ahead).wait_recv()
+            part[h, me] = part[h, me] + inbox[h, main, me].astype(jnp.float32)
+
+        kv = part[h, me, :, half_q:].astype(jnp.bfloat16)
+        first, second = kv[:, :size], kv[:, size:]
+        is_key = sub == 0
+        own = jnp.where(is_key, first, second)
+        kv_out[h] = jnp.where(is_key, second, first)
+        swap = send(kv_out.at[h], kv_in.at[h], kv_s.at[h], kv_r.at[h], sub=1 - sub)
+        swap.start()
+        for i in range(heads):
+            q_sum[:, i * size : (i + 1) * size] = turn(
+                part[h, me, :, i * size : (i + 1) * size].astype(jnp.bfloat16).astype(jnp.float32)
+            ).astype(jnp.bfloat16)
+        row = lax.broadcasted_iota(jnp.int32, (tokens, tokens), 0)
+        col = lax.broadcasted_iota(jnp.int32, (tokens, tokens), 1)
+        allowed = (col <= row) & (start_col[...] == start_row[...])
+        swap.wait_recv()
+        peer = kv_in[h]
+        keys = jnp.where(is_key, own, peer)
+        values = jnp.where(is_key, peer, own)
+        key_rot = turn(keys.astype(jnp.float32)).astype(jnp.bfloat16)
+        key_grad = jnp.zeros((tokens, size), jnp.float32)
+        value_grad = jnp.zeros((tokens, size), jnp.float32)
+        across = (((1,), (1,)), ((), ()))
+        down = (((0,), (0,)), ((), ()))
+        for i in range(heads):
+            cols = slice(i * size, (i + 1) * size)
+            query = q_sum[:, cols]
+            grad = grad_ref[:, h * half_q + i * size : h * half_q + (i + 1) * size]
+            scores = lax.dot_general(query, key_rot, across, preferred_element_type=jnp.float32)
+            scores = jnp.where(allowed, scores * scale, -jnp.inf)
+            weights = jnp.exp(scores - jnp.max(scores, axis=1, keepdims=True))
+            prob = weights / jnp.sum(weights, axis=1, keepdims=True)
+            grad_prob = lax.dot_general(grad, values, across, preferred_element_type=jnp.float32)
+            delta = jnp.sum(prob * grad_prob, axis=1, keepdims=True)
+            grad_score = (prob * (grad_prob - delta) * scale).astype(jnp.bfloat16)
+            grads[h, me, :, cols] = turn_back(
+                jnp.dot(grad_score, key_rot, preferred_element_type=jnp.float32)
+            ).astype(jnp.bfloat16)
+            key_grad += lax.dot_general(grad_score, query, down, preferred_element_type=jnp.float32)
+            value_grad += lax.dot_general(
+                prob.astype(jnp.bfloat16), grad, down, preferred_element_type=jnp.float32
+            )
+        key_grad = turn_back(key_grad).astype(jnp.bfloat16)
+        value_grad = value_grad.astype(jnp.bfloat16)
+        own = jnp.where(is_key, key_grad, value_grad)
+        dkv_out[h] = jnp.where(is_key, value_grad, key_grad)
+        swap = send(dkv_out.at[h], dkv_in.at[h], dkv_s.at[h], dkv_r.at[h], sub=1 - sub)
+        swap.start()
+        swap.wait_recv()
+        peer = dkv_in[h]
+        grads[h, me, :, half_q : half_q + size] = jnp.where(is_key, own, peer)
+        grads[h, me, :, half_q + size :] = jnp.where(is_key, peer, own)
+        spread(h, me, 0, ahead).start()
+
+        @pl.when(middle)
+        def _():
+            spread(h, me, 1, behind).start()
+
+    def spread(h, t, way, to):
+        return send(grads.at[h, t], grads.at[h, t], ag_s.at[h, t, way], ag_r.at[h, t], blk=to)
+
+    def relay(h, t, way, to):
+        @pl.when(middle)
+        def _():
+            spread(h, t, way, to).wait_recv()
+            spread(h, t, way, to).start()
+
+    def weight_grad(h):
+        @pl.loop(0, depth // tile)
+        def _(n):
+            cols = pl.ds(pl.multiple_of(n * tile, tile), tile)
+            total = lax.dot_general(
+                x_all[0, :, cols], grads[h, 0], (((0,), (0,)), ((), ())),
+                preferred_element_type=jnp.float32,
+            )
+            for t in range(1, 4):
+                total += lax.dot_general(
+                    x_all[t, :, cols], grads[h, t], (((0,), (0,)), ((), ())),
+                    preferred_element_type=jnp.float32,
+                )
+            total = total.astype(jnp.bfloat16)
+            dwq_ref[cols, h * half_q : (h + 1) * half_q] = total[:, :half_q]
+            dwkv_ref[cols, h * size : (h + 1) * size] = total[:, half_q : half_q + size]
+            dwkv_ref[cols, (h + 2) * size : (h + 3) * size] = total[:, half_q + size :]
+
+    def input_term(h, t, cols):
+        return lax.dot_general(
+            grads[h, t], w_all[h, cols, :], (((1,), (1,)), ((), ())),
+            preferred_element_type=jnp.float32,
+        )
+
+    def dx_copy(t, q):
+        return send(
+            dx_send.at[t], dx_in.at[q], dx_s.at[t], dx_r.at[q], tp=t // 2, sub=lax.rem(t, 2)
+        )
+
+    def input_block(t):
+        @pl.loop(0, depth // tile)
+        def _(n):
+            cols = pl.ds(pl.multiple_of(n * tile, tile), tile)
+            dx_send[t, :, cols] = (dx_part[t, :, cols] + input_term(1, t, cols)).astype(jnp.bfloat16)
+
+        @pl.when(t != share)
+        def _():
+            dx_copy(t, share).start()
+
+    for j in range(2):
+        pass_on(0, order[j], main, ahead)
+    pass_on(0, order[3], 1 - main, behind)
+    attend(0)
+    pass_on(1, order[0], main, ahead)
+    relay(0, order[3], 0, ahead)
+    pass_on(1, order[1], main, ahead)
+    relay(0, order[1], 1, behind)
+    pass_on(1, order[3], 1 - main, behind)
+    relay(0, order[0], 1, behind)
+    attend(1)
+
+    @pl.when(outer)
+    def _():
+        for j in (2, 1, 0):
+            spread(0, order[j], 0, ahead).wait_recv()
+
+    @pl.loop(0, 4)
+    def _(t):
+        @pl.loop(0, depth // tile)
+        def _(n):
+            cols = pl.ds(pl.multiple_of(n * tile, tile), tile)
+            dx_part[t, :, cols] = input_term(0, t, cols)
+
+    input_block(me)
+    weight_grad(0)
+
+    for mid_t, outer_t, way, to in (
+        (order[3], order[2], 0, ahead), (order[1], order[1], 1, behind), (order[0], order[0], 1, behind),
+    ):
+        relay(1, mid_t, way, to)
+
+        @pl.when(outer)
+        def _():
+            spread(1, outer_t, 0, ahead).wait_recv()
+
+        input_block(jnp.where(middle, mid_t, outer_t))
+
+    total = dx_send[share].astype(jnp.float32)
+    for q in mates:
+        dx_copy(share, q).wait_recv()
+        total += dx_in[q].astype(jnp.float32)
+    dx_sum[...] = total.astype(jnp.bfloat16)
+    home = send(
+        dx_sum, land, end_s, end_r, blk=share, tp=me // 2, sub=lax.rem(me, 2)
+    )
+
+    @pl.when(crossing)
+    def _():
+        home.start()
+
+    weight_grad(1)
+
+    @pl.when(crossing)
+    def _():
+        home.wait_recv()
+        dx_ref[...] = land[...]
+        home.wait_send()
+
+    @pl.when(jnp.logical_not(crossing))
+    def _():
+        dx_ref[...] = dx_sum[...]
+
+    for j in others:
+        x_first(j, me).wait_send()
+        for r in range(3):
+            fan(j, r, mates[r]).wait_send()
+    for h in range(2):
+        for j in range(2):
+            flow(h, order[j], main, ahead).wait_send()
+
+        @pl.when(outer)
+        def _():
+            flow(h, order[2], main, ahead).wait_send()
+
+        @pl.when(middle)
+        def _():
+            flow(h, order[3], main, ahead).wait_send()
+            spread(h, me, 1, behind).wait_send()
+            spread(h, order[3], 0, ahead).wait_send()
+            spread(h, order[1], 1, behind).wait_send()
+            spread(h, order[0], 1, behind).wait_send()
+
+        spread(h, me, 0, ahead).wait_send()
+        send(kv_out.at[h], kv_in.at[h], kv_s.at[h], kv_r.at[h], sub=1 - sub).wait_send()
+        send(dkv_out.at[h], dkv_in.at[h], dkv_s.at[h], dkv_r.at[h], sub=1 - sub).wait_send()
+    for q in mates:
+        dx_copy(q, share).wait_send()
+
+
+def fused(inputs, context_gradient, positions, query_weight, key_value_weight):
+    tokens = inputs.shape[0]
+    depth, query_cols = query_weight.shape
+    half_q = query_cols // 2
+    width = half_q + 2 * HEAD_SIZE
+    cosine_lookup, sine_lookup = rotary_tables(positions, HEAD_SIZE)
+    sign = jnp.where(jnp.arange(HEAD_SIZE) < HEAD_SIZE // 2, -1.0, 1.0).astype(jnp.float32)
+    starts = jnp.arange(tokens, dtype=jnp.int32) - positions
+    bf16, f32 = jnp.bfloat16, jnp.float32
+    dma = pltpu.SemaphoreType.DMA
+    vmem = pl.BlockSpec(memory_space=pltpu.VMEM)
+    grad_inputs, grad_query, grad_keyval = pl.pallas_call(
+        fused_kernel,
+        out_shape=(
+            jax.ShapeDtypeStruct((tokens, depth), bf16),
+            jax.ShapeDtypeStruct((depth, query_cols), bf16),
+            jax.ShapeDtypeStruct((depth, 4 * HEAD_SIZE), bf16),
+        ),
+        in_specs=[vmem] * 8,
+        out_specs=(vmem,) * 3,
+        scratch_shapes=[
+            pltpu.VMEM((2, depth, width), bf16),
+            pltpu.VMEM((4, tokens, depth), bf16),
+            pltpu.VMEM((2, 4, tokens, width), f32),
+            pltpu.VMEM((2, 4, tokens, width), bf16),
+            pltpu.VMEM((2, 2, 4, tokens, width), bf16),
+            pltpu.VMEM((tokens, half_q), bf16),
+            pltpu.VMEM((2, tokens, HEAD_SIZE), bf16),
+            pltpu.VMEM((2, tokens, HEAD_SIZE), bf16),
+            pltpu.VMEM((2, tokens, HEAD_SIZE), bf16),
+            pltpu.VMEM((2, tokens, HEAD_SIZE), bf16),
+            pltpu.VMEM((2, 4, tokens, width), bf16),
+            pltpu.VMEM((4, tokens, depth), f32),
+            pltpu.VMEM((4, tokens, depth), bf16),
+            pltpu.VMEM((4, tokens, depth), bf16),
+            pltpu.VMEM((tokens, depth), bf16),
+            pltpu.VMEM((tokens, depth), bf16),
+            dma((4,)), dma((4,)), dma((4, 3)), dma((4, 3)), dma((2, 4)), dma((2, 2, 4)),
+            dma((2,)), dma((2,)), dma((2,)), dma((2,)), dma((2, 4, 2)), dma((2, 4)),
+            dma((4,)), dma((4,)), dma, dma,
+        ],
+        compiler_params=pltpu.CompilerParams(
+            collective_id=0, has_side_effects=True, vmem_limit_bytes=60 * 1024 * 1024
+        ),
+    )(
+        inputs, context_gradient, starts[:, None], starts[None, :], cosine_lookup,
+        sine_lookup * sign, query_weight, key_value_weight.reshape(depth, -1),
+    )
+    return (grad_inputs, grad_query, grad_keyval.reshape(depth, 1, -1))
+
+
 def on_device(inputs, context_gradient, positions, query_weight, key_value_weight):
     tok_rows = inputs.shape[0]
     block_rows = query_weight.shape[0]
     query_cols = query_weight.shape[1]
     local_heads = query_cols // HEAD_SIZE
     local_groups = key_value_weight.shape[2] // HEAD_SIZE
+    sizes = tuple(lax.axis_size(axis) for axis in ("blk", "tp", "sub"))
+    if sizes == (4, 2, 2) and (local_heads, local_groups) == (2 * QUERY_PER_GROUP, 4):
+        return fused(inputs, context_gradient, positions, query_weight, key_value_weight)
     pair_index = lax.axis_index("sub")
     blocks = lax.axis_size("blk")
     sharers = lax.axis_size("tp") * lax.axis_size("sub")

time: 295 us -> 176 us (0.60)
  Pallas kernels: 0 us -> 166 us
  waiting for transfers between devices: 151 us -> 0 us
  blocking collectives: 48.1 us -> 0 us
  matrix products: 47.7 us -> 0 us
  between operations: 14.5 us -> 0.66 us
  local copies, waits for them, and re-layouts: 17.1 us -> 6.81 us
  other arithmetic: 11.6 us -> 2.12 us
  starting transfers between devices: 4.27 us -> 0 us
    pallas_call x0 -> x1, Pallas kernels: none -> 166 us  [fused(): pl.pallas_call(fused_kernel, out_shape=(jax.ShapeDtypeStruct((tokens, dep...]
    ppermute x9 -> x0, waiting for transfers between devices: 130 us -> none  [the longest x6 114 us: passed_along(): return lax.ppermute(value, axis, pairs)]
    all_to_all x2 -> x0, blocking collectives: 48.1 us -> none  [the longest x1 28.9 us: on_device(): lax.all_to_all(partial_inputs.reshape(sharers, -1, block_rows), ('tp', 's...]
    dot_general x14 -> x0, matrix products: 44.5 us -> none  [the longest x4 13.7 us: projection_term(): return jnp.dot(rows, weight_cols, preferred_element_type=jnp.float32)]
    all_gather x1 -> x0, waiting for transfers between devices: 20.7 us -> none  [on_device(): columns = lax.all_gather(shared, ('tp', 'sub'), axis=1, tiled=True)]
    convert_element_type x6 -> x0, other arithmetic: 5.61 us -> none  [the longest x2 1.32 us: ring_sum(): total = block.astype(jnp.bfloat16)]
    ppermute x9 -> x0, starting transfers between devices: 4.23 us -> none  [the longest x1 1.92 us: on_device(): grad_inputs = lax.ppermute(grad_inputs, ('blk', 'tp', 'sub'), swaps)]
    reshape x4 -> x0, local copies, waits for them, and re-layouts: 3.33 us -> none  [the longest x1 1.25 us: on_device(): query_gradient_rows = inverse_rotation(grad_query, cosine_lookup, sine_lo...]
  transfers between devices with their start and end apart: 10 -> 0, of which waited for: 8 -> 0; matrix products, arithmetic and copies ran while one was open for 8% -> 0% of each run, Pallas kernels for 0% -> 0%
where the time goes in v2:
time: 176 us
  Pallas kernels  166 us (94%)
  local copies, waits for them, and re-layouts  6.81 us (4%)
  other arithmetic  2.12 us (1%)
    pallas_call x1, Pallas kernels, fused(): pl.pallas_call(fused_kernel, out_shape=(jax.ShapeDtypeStruct((tokens, dep...  166 us
    unnamed x7, local copies, waits for them, and re-layouts  6.01 us

profile of v2, /device:TPU:2, one launch (start us, length us, event | category | flops | bytes accessed | tf_op | source)
XLA Modules:
  0.0 175.7 jit_solution(9730266423824275889)
XLA Ops:
  0.7 0.8 fusion
  1.4 0.0 copy-start.1
  1.4 0.8 copy.8.start_col
  2.2 0.5 multiply_sine_fusion
  2.8 0.8 pad_maximum_fusion
  3.6 0.0 copy-done.1
  3.6 166.1 %shard_map.76 = (bf16[256,1024]{1,0:T(8,128)(2,1)}, bf16[1024,1024]{1,0:T(8,128)(2,1)}, bf16[1024,512]{1,0:T(8,128)(2,1)}) custom-call(bf16[256,4096]{1,0:T(8,128)(2,1)} %x_ref.1, bf16[256,1024]{1,0:T(8,128)(2,1)} %grad_ref.1, s32[256,1]{1,0:T(8,128)} %copy.8.start_col, s32[1,256]{1,0:T(1,128)} %bitcast.7, f32[256,128]{1,0:T(8,128)} %get-tuple-element.13.cos_ref, ...), custom_call_target="tpu_custom_call" | custom-call | tf_op jit(solution)/shard_map/pallas_call | solution.py:459
  169.7 1.9 %copy.12 = bf16[256,1024]{1,0:T(8,128)(2,1)} copy(bf16[256,1024]{1,0:T(8,128)(2,1)} %get-tuple-element.18) | data formatting | bytes 1048576
  171.6 0.0 copy-start
  171.6 3.2 %copy.13 = bf16[1024,1024]{1,0:T(8,128)(2,1)} copy(bf16[1024,1024]{1,0:T(8,128)(2,1)} %get-tuple-element.19) | data formatting | bytes 4194304
  174.7 0.0 copy-done
  174.7 1.0 copy.14
  (2 shorter events, 0.0 us)
Async XLA Ops:
  1.4 2.2 %copy-start.1 = (s32[256]{0:T(256)}, s32[256]{0:T(256)S(1)}, u32[]{:S(2)}) copy-start(s32[256]{0:T(256)S(1)} %get-tuple-element.12) | copy-start | bytes 3076
  171.6 3.2 %copy-start = (bf16[1024,512]{1,0:T(8,128)(2,1)S(1)}, bf16[1024,512]{1,0:T(8,128)(2,1)}, u32[]{:S(2)}) copy-start(bf16[1024,512]{1,0:T(8,128)(2,1)} %get-tuple-element.8) | copy-start | bytes 3145732

commit v3 on v2

--- a/solution.py
+++ b/solution.py
@@ -2,6 +2,7 @@
 
 import jax
 import jax.numpy as jnp
+import numpy as np
 from jax import lax
 from jax.experimental import pallas as pl
 from jax.experimental.pallas import tpu as pltpu
@@ -104,11 +105,11 @@
 
 
 def fused_kernel(
-    x_ref, grad_ref, start_col, start_row, cos_ref, sin_ref, wq_ref, wkv_ref,
+    x_ref, grad_hbm, pos_ref, freq_ref, sign_ref, wq_ref, wkv_ref,
     dx_ref, dwq_ref, dwkv_ref,
     w_all, x_all, part, sends, inbox, q_sum, kv_out, kv_in, dkv_out, dkv_in, grads, dx_part,
-    dx_send, dx_in, dx_sum, land,
-    x_s, x_r, fan_s, fan_r, flow_s, flow_r, kv_s, kv_r, dkv_s, dkv_r, ag_s, ag_r, dx_s, dx_r, end_s, end_r,
+    pair_send, pair_in, own_sum, side_send, side_in, land, cos_ref, sin_ref, grad_ref, load_s,
+    x_s, x_r, fan_s, fan_r, flow_s, flow_r, kv_s, kv_r, dkv_s, dkv_r, ag_s, ag_r, dx_s, dx_r, end_s, end_r, pair_s, pair_r,
 ):
     size = HEAD_SIZE
     half_q = wq_ref.shape[1] // 2
@@ -137,6 +138,10 @@
             device_id=where, device_id_type=pl.DeviceIdType.MESH,
         )
 
+    def apart(blk, x, core):
+        same_line = (x == tp) & (core == sub)
+        return jnp.logical_not(same_line | (blk == me))
+
     barrier = pltpu.get_barrier_semaphore()
     for j in others:
         pl.semaphore_signal(barrier, inc=1, device_id={"blk": j}, device_id_type=pl.DeviceIdType.MESH)
@@ -145,17 +150,18 @@
             barrier, inc=1, device_id={"tp": q // 2, "sub": lax.rem(q, 2)},
             device_id_type=pl.DeviceIdType.MESH,
         )
-    crossing = me != share
-
-    @pl.when(crossing)
-    def _():
-        pl.semaphore_signal(
-            barrier, inc=1,
-            device_id={"blk": share, "tp": me // 2, "sub": lax.rem(me, 2)},
-            device_id_type=pl.DeviceIdType.MESH,
-        )
-
-    pl.semaphore_wait(barrier, 6 + jnp.where(crossing, 1, 0))
+    def greet(where, needed):
+        @pl.when(needed)
+        def _():
+            pl.semaphore_signal(barrier, inc=1, device_id=where, device_id_type=pl.DeviceIdType.MESH)
+
+    expected = 6
+    for i in range(2):
+        target = 2 * tp + i
+        needed = apart(target, me // 2, lax.rem(me, 2))
+        expected += jnp.where(needed, 1, 0)
+        greet({"blk": share, "tp": me // 2, "sub": i}, apart(share, me // 2, i))
+    pl.semaphore_wait(barrier, expected)
 
     my_rows = pl.ds(pl.multiple_of(share * share_rows, share_rows), share_rows)
 
@@ -171,11 +177,24 @@
     for j in others:
         x_first(j, me).start()
 
-    x_all[me] = x_ref[:, pl.ds(pl.multiple_of(me * depth, depth), depth)]
+    loads = [
+        (x_ref.at[:, pl.ds(pl.multiple_of(me * depth, depth), depth)], x_all.at[me]),
+        (grad_hbm, grad_ref),
+    ]
     for h in range(2):
-        w_all[h, :, :half_q] = wq_ref[:, h * half_q : (h + 1) * half_q]
-        w_all[h, :, half_q : half_q + size] = wkv_ref[:, h * size : (h + 1) * size]
-        w_all[h, :, half_q + size :] = wkv_ref[:, (h + 2) * size : (h + 3) * size]
+        loads += [
+            (wq_ref.at[:, h * half_q : (h + 1) * half_q], w_all.at[h, :, :half_q]),
+            (wkv_ref.at[:, h * size : (h + 1) * size], w_all.at[h, :, half_q : half_q + size]),
+            (wkv_ref.at[:, (h + 2) * size : (h + 3) * size], w_all.at[h, :, half_q + size :]),
+        ]
+    loads = [pltpu.make_async_copy(a, b, load_s.at[i]) for i, (a, b) in enumerate(loads)]
+    for load in loads:
+        load.start()
+
+    places = jnp.broadcast_to(pos_ref[...].astype(jnp.float32), (size, tokens)).T
+    angles = places * freq_ref[...]
+    cos_ref[...] = jnp.cos(angles)
+    sin_ref[...] = jnp.sin(angles) * sign_ref[...]
 
     def fan(t, r, q):
         return send(
@@ -187,6 +206,9 @@
         x_first(t, t).wait_recv()
         for r in range(3):
             fan(t, r, mates[r]).start()
+
+    for load in loads:
+        load.wait()
 
     def fan_wait(t):
         for r in range(3):
@@ -208,6 +230,12 @@
             part[h, d, :, cols] = jnp.dot(
                 x_all[d], w_all[h, :, cols], preferred_element_type=jnp.float32
             )
+
+    def emit(h, j):
+        sends[h, order[j]] = part[h, order[j]].astype(jnp.bfloat16)
+        if h + j > 0:
+            flow(0 if j == 0 else h, order[(j + 2) % 3], main, ahead).wait_send()
+        flow(h, order[j], main, ahead).start()
 
     for h in range(2):
         for j in range(4):
@@ -217,11 +245,14 @@
                 def _():
                     fan_wait(d)
             project(h, d)
-            if j < 3:
+            if h == 0 and j < 3:
                 @pl.when(outer)
                 def _():
-                    sends[h, d] = part[h, d].astype(jnp.bfloat16)
-                    flow(h, d, main, ahead).start()
+                    emit(0, j)
+
+    @pl.when(outer)
+    def _():
+        emit(1, 0)
 
     def pass_on(h, d, way, to):
         @pl.when(middle)
@@ -263,7 +294,8 @@
             ).astype(jnp.bfloat16)
         row = lax.broadcasted_iota(jnp.int32, (tokens, tokens), 0)
         col = lax.broadcasted_iota(jnp.int32, (tokens, tokens), 1)
-        allowed = (col <= row) & (start_col[...] == start_row[...])
+        starts = (col - pos_ref[...]).astype(jnp.float32)
+        allowed = (col <= row) & (starts == starts.T)
         swap.wait_recv()
         peer = kv_in[h]
         keys = jnp.where(is_key, own, peer)
@@ -340,25 +372,75 @@
             preferred_element_type=jnp.float32,
         )
 
-    def dx_copy(t, q):
+    half_d = depth // 2
+    mine = pl.ds(pl.multiple_of(sub * half_d, half_d), half_d)
+    theirs = pl.ds(pl.multiple_of((1 - sub) * half_d, half_d), half_d)
+    home_x, home_sub = me // 2, lax.rem(me, 2)
+
+    def pair_copy(t):
+        return send(pair_send.at[t], pair_in.at[t], pair_s.at[t], pair_r.at[t], sub=1 - sub)
+
+    def side_copy(t):
+        return send(side_send.at[t], side_in.at[t], dx_s.at[t], dx_r.at[t], tp=1 - tp)
+
+    def home_copy(t, i, where_t):
         return send(
-            dx_send.at[t], dx_in.at[q], dx_s.at[t], dx_r.at[q], tp=t // 2, sub=lax.rem(t, 2)
+            side_send.at[t], land.at[:, pl.ds(pl.multiple_of(i * half_d, half_d), half_d)],
+            end_s.at[t], end_r.at[i], blk=where_t, tp=home_x, sub=home_sub,
         )
 
+    def stays(t):
+        return (t == me) & (sub == home_sub)
+
+    def finish(t):
+        @pl.when(t // 2 == tp)
+        def _():
+            side_copy(t).wait_recv()
+            side_send[t] = (own_sum[t] + side_in[t].astype(jnp.float32)).astype(jnp.bfloat16)
+
+            @pl.when(stays(t))
+            def _():
+                land[:, mine] = side_send[t]
+
+            @pl.when(jnp.logical_not(stays(t)))
+            def _():
+                home_copy(t, sub, t).start()
+
     def input_block(t):
-        @pl.loop(0, depth // tile)
+        @pl.loop(0, half_d // tile)
         def _(n):
+            there = pl.ds(pl.multiple_of((1 - sub) * half_d + n * tile, tile), tile)
             cols = pl.ds(pl.multiple_of(n * tile, tile), tile)
-            dx_send[t, :, cols] = (dx_part[t, :, cols] + input_term(1, t, cols)).astype(jnp.bfloat16)
-
-        @pl.when(t != share)
-        def _():
-            dx_copy(t, share).start()
+            pair_send[t, :, cols] = (dx_part[t, :, there] + input_term(1, t, there)).astype(
+                jnp.bfloat16
+            )
+
+        pair_copy(t).start()
+
+        @pl.loop(0, half_d // tile)
+        def _(n):
+            here = pl.ds(pl.multiple_of(sub * half_d + n * tile, tile), tile)
+            cols = pl.ds(pl.multiple_of(n * tile, tile), tile)
+            own_sum[t, :, cols] = dx_part[t, :, here] + input_term(1, t, here)
+
+        pair_copy(t).wait_recv()
+        own_sum[t] = own_sum[t] + pair_in[t].astype(jnp.float32)
+
+        @pl.when(t // 2 != tp)
+        def _():
+            side_send[t] = own_sum[t].astype(jnp.bfloat16)
+            side_copy(t).start()
 
     for j in range(2):
         pass_on(0, order[j], main, ahead)
     pass_on(0, order[3], 1 - main, behind)
     attend(0)
+
+    @pl.when(outer)
+    def _():
+        emit(1, 1)
+        emit(1, 2)
+
     pass_on(1, order[0], main, ahead)
     relay(0, order[3], 0, ahead)
     pass_on(1, order[1], main, ahead)
@@ -381,6 +463,7 @@
 
     input_block(me)
     weight_grad(0)
+    previous = me
 
     for mid_t, outer_t, way, to in (
         (order[3], order[2], 0, ahead), (order[1], order[1], 1, behind), (order[0], order[0], 1, behind),
@@ -391,47 +474,45 @@
         def _():
             spread(1, outer_t, 0, ahead).wait_recv()
 
-        input_block(jnp.where(middle, mid_t, outer_t))
-
-    total = dx_send[share].astype(jnp.float32)
-    for q in mates:
-        dx_copy(share, q).wait_recv()
-        total += dx_in[q].astype(jnp.float32)
-    dx_sum[...] = total.astype(jnp.bfloat16)
-    home = send(
-        dx_sum, land, end_s, end_r, blk=share, tp=me // 2, sub=lax.rem(me, 2)
-    )
-
-    @pl.when(crossing)
-    def _():
-        home.start()
-
+        latest = jnp.where(middle, mid_t, outer_t)
+        input_block(latest)
+        finish(previous)
+        previous = latest
+
+    finish(previous)
     weight_grad(1)
 
-    @pl.when(crossing)
-    def _():
-        home.wait_recv()
-        dx_ref[...] = land[...]
-        home.wait_send()
-
-    @pl.when(jnp.logical_not(crossing))
-    def _():
-        dx_ref[...] = dx_sum[...]
+    for i in range(2):
+        @pl.when(jnp.logical_not((share == me) & (sub == i)))
+        def _():
+            home_copy(me, i, me).wait_recv()
+
+    dx_ref[...] = land[...]
+    for t in range(4):
+        pair_copy(t).wait_send()
+
+        @pl.when(t // 2 != tp)
+        def _():
+            side_copy(t).wait_send()
+
+        @pl.when((t // 2 == tp) & jnp.logical_not(stays(t)))
+        def _():
+            home_copy(t, sub, t).wait_send()
 
     for j in others:
         x_first(j, me).wait_send()
         for r in range(3):
             fan(j, r, mates[r]).wait_send()
     for h in range(2):
-        for j in range(2):
-            flow(h, order[j], main, ahead).wait_send()
-
-        @pl.when(outer)
-        def _():
-            flow(h, order[2], main, ahead).wait_send()
+        if h == 1:
+            @pl.when(outer)
+            def _():
+                flow(h, order[2], main, ahead).wait_send()
 
         @pl.when(middle)
         def _():
+            for j in range(2):
+                flow(h, order[j], main, ahead).wait_send()
             flow(h, order[3], main, ahead).wait_send()
             spread(h, me, 1, behind).wait_send()
             spread(h, order[3], 0, ahead).wait_send()
@@ -441,8 +522,6 @@
         spread(h, me, 0, ahead).wait_send()
         send(kv_out.at[h], kv_in.at[h], kv_s.at[h], kv_r.at[h], sub=1 - sub).wait_send()
         send(dkv_out.at[h], dkv_in.at[h], dkv_s.at[h], dkv_r.at[h], sub=1 - sub).wait_send()
-    for q in mates:
-        dx_copy(q, share).wait_send()
 
 
 def fused(inputs, context_gradient, positions, query_weight, key_value_weight):
@@ -450,12 +529,14 @@
     depth, query_cols = query_weight.shape
     half_q = query_cols // 2
     width = half_q + 2 * HEAD_SIZE
-    cosine_lookup, sine_lookup = rotary_tables(positions, HEAD_SIZE)
-    sign = jnp.where(jnp.arange(HEAD_SIZE) < HEAD_SIZE // 2, -1.0, 1.0).astype(jnp.float32)
-    starts = jnp.arange(tokens, dtype=jnp.int32) - positions
+    half = np.arange(HEAD_SIZE // 2, dtype=np.float64)
+    frequency = np.exp(half * (-2.0 * math.log(ROPE_BASE) / HEAD_SIZE)).astype(np.float32)
+    frequency = np.concatenate([frequency, frequency])[None, :]
+    sign = np.where(np.arange(HEAD_SIZE) < HEAD_SIZE // 2, -1.0, 1.0).astype(np.float32)[None, :]
     bf16, f32 = jnp.bfloat16, jnp.float32
     dma = pltpu.SemaphoreType.DMA
     vmem = pl.BlockSpec(memory_space=pltpu.VMEM)
+    whole = pl.BlockSpec(memory_space=pl.ANY)
     grad_inputs, grad_query, grad_keyval = pl.pallas_call(
         fused_kernel,
         out_shape=(
@@ -463,7 +544,7 @@
             jax.ShapeDtypeStruct((depth, query_cols), bf16),
             jax.ShapeDtypeStruct((depth, 4 * HEAD_SIZE), bf16),
         ),
-        in_specs=[vmem] * 8,
+        in_specs=[whole, whole] + [vmem] * 3 + [whole, whole],
         out_specs=(vmem,) * 3,
         scratch_shapes=[
             pltpu.VMEM((2, depth, width), bf16),
@@ -478,20 +559,25 @@
             pltpu.VMEM((2, tokens, HEAD_SIZE), bf16),
             pltpu.VMEM((2, 4, tokens, width), bf16),
             pltpu.VMEM((4, tokens, depth), f32),
-            pltpu.VMEM((4, tokens, depth), bf16),
-            pltpu.VMEM((4, tokens, depth), bf16),
+            pltpu.VMEM((4, tokens, depth // 2), bf16),
+            pltpu.VMEM((4, tokens, depth // 2), bf16),
+            pltpu.VMEM((4, tokens, depth // 2), f32),
+            pltpu.VMEM((4, tokens, depth // 2), bf16),
+            pltpu.VMEM((4, tokens, depth // 2), bf16),
             pltpu.VMEM((tokens, depth), bf16),
-            pltpu.VMEM((tokens, depth), bf16),
+            pltpu.VMEM((tokens, HEAD_SIZE), f32),
+            pltpu.VMEM((tokens, HEAD_SIZE), f32),
+            pltpu.VMEM((tokens, query_cols), bf16),
+            dma((8,)),
             dma((4,)), dma((4,)), dma((4, 3)), dma((4, 3)), dma((2, 4)), dma((2, 2, 4)),
             dma((2,)), dma((2,)), dma((2,)), dma((2,)), dma((2, 4, 2)), dma((2, 4)),
-            dma((4,)), dma((4,)), dma, dma,
+            dma((4,)), dma((4,)), dma((4,)), dma((2,)), dma((4,)), dma((4,)),
         ],
         compiler_params=pltpu.CompilerParams(
             collective_id=0, has_side_effects=True, vmem_limit_bytes=60 * 1024 * 1024
         ),
     )(
-        inputs, context_gradient, starts[:, None], starts[None, :], cosine_lookup,
-        sine_lookup * sign, query_weight, key_value_weight.reshape(depth, -1),
+        inputs, context_gradient, positions[None, :], frequency, sign, query_weight, key_value_weight.reshape(depth, -1),
     )
     return (grad_inputs, grad_query, grad_keyval.reshape(depth, 1, -1))
 

time: 176 us -> 171 us (0.972); the launches traced: 176 us -> 169 us
  Pallas kernels: 166 us -> 162 us
  other arithmetic: 2.12 us -> 0 us
    pallas_call x1, Pallas kernels: 166 us -> 162 us  [fused(): pl.pallas_call(fused_kernel, out_shape=(jax.ShapeDtypeStruct((tokens, dep...]
    unnamed x7 -> x5, local copies, waits for them, and re-layouts: 6.01 us -> 6.01 us
where the time goes in v3:
time: 171 us; the launch traced here: 169 us
  Pallas kernels  162 us (95%)
  local copies, waits for them, and re-layouts  6.01 us (4%)
    pallas_call x1, Pallas kernels, fused(): pl.pallas_call(fused_kernel, out_shape=(jax.ShapeDtypeStruct((tokens, dep...  162 us
    unnamed x5, local copies, waits for them, and re-layouts  6.01 us

profile of v3, /device:TPU:2, one launch (start us, length us, event | category | flops | bytes accessed | tf_op | source)
XLA Modules:
  0.0 168.8 jit_solution(11142381522528756972)
XLA Ops:
  0.6 162.2 %shard_map.94 = (bf16[256,1024]{1,0:T(8,128)(2,1)}, bf16[1024,1024]{1,0:T(8,128)(2,1)}, bf16[1024,512]{1,0:T(8,128)(2,1)}) custom-call(bf16[256,4096]{1,0:T(8,128)(2,1)} %x_ref.1, bf16[256,1024]{1,0:T(8,128)(2,1)} %grad_hbm.1, s32[1,256]{1,0:T(1,128)} %bitcast.5, f32[1,128]{1,0:T(1,128)} %constant.4.clone.freq_ref, f32[1,128]{1,0:T(1,128)} %constant.5.clone.sign_ref, ...), custom_call_target="tpu_custom_call" | custom-call | tf_op jit(solution)/shard_map/pallas_call | solution.py:540
  162.8 1.9 %copy.13 = bf16[256,1024]{1,0:T(8,128)(2,1)} copy(bf16[256,1024]{1,0:T(8,128)(2,1)} %get-tuple-element.12) | data formatting | bytes 1048576
  164.7 0.0 copy-start
  164.7 3.2 %copy.14 = bf16[1024,1024]{1,0:T(8,128)(2,1)} copy(bf16[1024,1024]{1,0:T(8,128)(2,1)} %get-tuple-element.13) | data formatting | bytes 4194304
  167.9 0.0 copy-done
  167.9 1.0 copy.15
Async XLA Ops:
  164.7 3.2 %copy-start = (bf16[1024,512]{1,0:T(8,128)(2,1)S(1)}, bf16[1024,512]{1,0:T(8,128)(2,1)}, u32[]{:S(2)}) copy-start(bf16[1024,512]{1,0:T(8,128)(2,1)} %get-tuple-element.8) | copy-start | bytes 3145732

commit v4 on v3

--- a/solution.py
+++ b/solution.py
@@ -196,27 +196,28 @@
     cos_ref[...] = jnp.cos(angles)
     sin_ref[...] = jnp.sin(angles) * sign_ref[...]
 
-    def fan(t, r, q):
+    def fan(t, kind, row_tp, row_sub):
+        rows = rows_of(row_tp * 2 + row_sub)
+        where = {"tp": 1 - tp} if kind == 1 else {"sub": 1 - sub}
         return send(
-            x_all.at[t, my_rows, :], x_all.at[t, my_rows, :], fan_s.at[t, r], fan_r.at[t, r],
-            tp=q // 2, sub=lax.rem(q, 2),
+            x_all.at[t, rows, :], x_all.at[t, rows, :], fan_s.at[t, kind], fan_r.at[t, kind], **where
         )
 
-    for t in others:
+    def fan_own(t):
         x_first(t, t).wait_recv()
-        for r in range(3):
-            fan(t, r, mates[r]).start()
+        fan(t, 1, tp, sub).start()
+        fan(t, 0, tp, sub).start()
+
+    def fan_side(t):
+        fan(t, 1, 1 - tp, sub).wait_recv()
+        fan(t, 2, 1 - tp, sub).start()
 
     for load in loads:
         load.wait()
 
     def fan_wait(t):
-        for r in range(3):
-            q = lax.rem(share + 3 - r, 4)
-            send(
-                x_all.at[t, rows_of(q), :], x_all.at[t, rows_of(q), :], fan_s.at[t, r],
-                fan_r.at[t, r], tp=q // 2, sub=lax.rem(q, 2),
-            ).wait_recv()
+        fan(t, 0, tp, 1 - sub).wait_recv()
+        fan(t, 2, 1 - tp, 1 - sub).wait_recv()
 
     def flow(h, d, way, to):
         return send(sends.at[h, d], inbox.at[h, way, d], flow_s.at[h, d], flow_r.at[h, way, d], blk=to)
@@ -241,6 +242,16 @@
         for j in range(4):
             d = order[j]
             if h == 0:
+                if j == 0:
+                    fan_own(others[0])
+                    fan_own(others[1])
+                    fan_side(others[0])
+                elif j == 1:
+                    fan_own(others[2])
+                    fan_side(others[1])
+                elif j == 2:
+                    fan_side(others[2])
+
                 @pl.when(d != me)
                 def _():
                     fan_wait(d)
@@ -501,8 +512,9 @@
 
     for j in others:
         x_first(j, me).wait_send()
-        for r in range(3):
-            fan(j, r, mates[r]).wait_send()
+        fan(j, 0, tp, sub).wait_send()
+        fan(j, 1, tp, sub).wait_send()
+        fan(j, 2, 1 - tp, sub).wait_send()
     for h in range(2):
         if h == 1:
             @pl.when(outer)

time: 171 us -> 167 us (0.977)
  the two profiles are of different devices: /device:TPU:2 before, /device:TPU:3 now
where the time goes in v4:
time: 167 us
  Pallas kernels  160 us (96%)
  local copies, waits for them, and re-layouts  6.01 us (4%)
    pallas_call x1, Pallas kernels, fused(): pl.pallas_call(fused_kernel, out_shape=(jax.ShapeDtypeStruct((tokens, dep...  160 us
    unnamed x5, local copies, waits for them, and re-layouts  6.01 us

profile of v4, /device:TPU:3, one launch (start us, length us, event | category | flops | bytes accessed | tf_op | source)
XLA Modules:
  0.0 166.7 jit_solution(3184038761610536287)
XLA Ops:
  0.6 160.0 %shard_map.94 = (bf16[256,1024]{1,0:T(8,128)(2,1)}, bf16[1024,1024]{1,0:T(8,128)(2,1)}, bf16[1024,512]{1,0:T(8,128)(2,1)}) custom-call(bf16[256,4096]{1,0:T(8,128)(2,1)} %x_ref.1, bf16[256,1024]{1,0:T(8,128)(2,1)} %grad_hbm.1, s32[1,256]{1,0:T(1,128)} %bitcast.5, f32[1,128]{1,0:T(1,128)} %constant.4.clone.freq_ref, f32[1,128]{1,0:T(1,128)} %constant.5.clone.sign_ref, ...), custom_call_target="tpu_custom_call" | custom-call | tf_op jit(solution)/shard_map/pallas_call | solution.py:552
  160.7 1.9 %copy.13 = bf16[256,1024]{1,0:T(8,128)(2,1)} copy(bf16[256,1024]{1,0:T(8,128)(2,1)} %get-tuple-element.12) | data formatting | bytes 1048576
  162.6 0.0 copy-start
  162.6 3.2 %copy.14 = bf16[1024,1024]{1,0:T(8,128)(2,1)} copy(bf16[1024,1024]{1,0:T(8,128)(2,1)} %get-tuple-element.13) | data formatting | bytes 4194304
  165.7 0.0 copy-done
  165.7 1.0 copy.15
Async XLA Ops:
  162.6 3.2 %copy-start = (bf16[1024,512]{1,0:T(8,128)(2,1)S(1)}, bf16[1024,512]{1,0:T(8,128)(2,1)}, u32[]{:S(2)}) copy-start(bf16[1024,512]{1,0:T(8,128)(2,1)} %get-tuple-element.8) | copy-start | bytes 3145732
